TPU v7x, 32 devices: a whole 2x2x4 slice. The times are simulated.
32 devices in a mesh: front: 2 (over core), grid: 4 (over y, x), depth: 4 (over z).
Axes of the slice: x: 2, y: 2, z: 4, core: 2. Of those that a mesh axis runs over, the one named last changes fastest.
Arguments:
- panel_base: float32 [2, 4, 4, 256, 256], P('front', None, 'grid'), as said below
- slab_base: float32 [2, 4, 4, 256, 1024], P('front', None, 'grid', None, 'depth'), may hold values from -6 to 6
- child_tiles: float32 [2, 4, 4, 4, 256, 256], P('front', 'grid', 'depth'), may hold values from -3 to 3
- child_maps: int32 [2, 4, 4, 4, 2], P('front', 'grid', 'depth'), may hold values from 0 to 15, as said below
- front_orders: int32 [2], P('front'), may hold values from 1280 to 4096, as said below
Outputs:
- panel_factor: float32 [2, 4, 4, 256, 256], P('front', None, 'grid')
- schur: float32 [2, 4, 4, 256, 1024], P('front', None, 'grid', None, 'depth')
Inputs may be any that keep to these rules, and one draw needn't show every extreme that they name: Rows r = 0, g = 0 of each front's panel_base form a symmetric positive definite tile. `child_maps`: entry 0 is a parent tile row, entry 1 a tile column from 0 to 4, never both 0. A tile's owner is its parent tile row modulo 4; among one device's 4 tiles at most 2 have the same owner, and in every front one owner receives exactly 2 tiles from every device. `front_orders`: A multiple of 256; in every draw some front has the order 4096.
All inputs are finite; a program needn't handle non-finite values.
Results may differ from a plain program's by a relative error of at most 0.0003.
Values sent between devices are 32-bit elements; how exact they have to be, the bound alone decides.
A program may use at most 64 MiB of HBM per device.

v0:
```python
import jax
import jax.numpy as jnp
from jax import lax
from jax.sharding import PartitionSpec as P

CAP = 2


def from_root(x, axis, root):
    mine = lax.axis_index(axis) == root
    return lax.psum(jnp.where(mine, x, jnp.zeros_like(x)), axis)


def on_device(panel_base, slab_base, child_tiles, child_maps, front_orders):
    grid_size = lax.axis_size("grid")
    depth_size = lax.axis_size("depth")
    grid_pos = lax.axis_index("grid")
    depth_pos = lax.axis_index("depth")
    fronts_here = panel_base.shape[0]
    rounds = panel_base.shape[1]
    tile_size = panel_base.shape[3]
    column_share = slab_base.shape[4] // tile_size
    next_tiles = column_share * depth_size
    positions = rounds * (next_tiles + 1)
    tile_maps = child_maps[:, 0, 0]
    tile_data = child_tiles[:, 0, 0]
    kid_count = tile_data.shape[1]
    parent_row = tile_maps[..., 0]
    parent_col = tile_maps[..., 1]
    owners = parent_row % grid_size
    same_owner = owners[:, :, None] == owners[:, None, :]
    earlier = jnp.arange(kid_count)[None, :] < jnp.arange(kid_count)[:, None]
    bucket_slot = jnp.sum((same_owner & earlier[None]).astype(jnp.int32), axis=2)
    destination = owners * CAP + bucket_slot
    routing = (destination[:, None, :] == jnp.arange(grid_size * CAP)[None, :, None]).astype(
        jnp.float32
    )
    send_tiles = jnp.einsum("fsk,fkab->fsab", routing, tile_data, precision=lax.Precision.HIGHEST)
    send_tiles = send_tiles.reshape(fronts_here, grid_size, CAP, tile_size, tile_size)
    position = parent_row // grid_size * (next_tiles + 1) + parent_col
    placing = (position[..., None] == jnp.arange(positions)[None, None, :]).astype(jnp.float32)
    send_places = jnp.einsum("fsk,fkp->fsp", routing, placing, precision=lax.Precision.HIGHEST)
    send_places = send_places.reshape(fronts_here, grid_size, CAP, positions)
    arrived, arrived_places = (
        lax.all_to_all(send_tiles, "grid", split_axis=1, concat_axis=1, tiled=True),
        lax.all_to_all(send_places, "grid", split_axis=1, concat_axis=1, tiled=True),
    )
    partial_value = jnp.einsum(
        "fskp,fskab->fpab", arrived_places, arrived, precision=lax.Precision.HIGHEST
    )
    partial_value = partial_value.reshape(fronts_here, rounds, next_tiles + 1, tile_size, tile_size)
    panel_part = partial_value[:, :, 0]
    slab_part = partial_value[:, :, 1:]
    panel_sum, slab_sum = lax.psum((panel_part, slab_part), "depth")
    slab_mine = lax.dynamic_slice_in_dim(slab_sum, depth_pos * column_share, column_share, 2)
    tile_index = jnp.arange(rounds) * grid_size + grid_pos
    live_rows = ((tile_index * tile_size)[None, :] < front_orders[:, None]).astype(jnp.float32)
    front_panel = (panel_base[:, :, 0] + panel_sum) * live_rows[:, :, None, None]
    slab_cols = slab_mine.transpose(0, 1, 3, 2, 4).reshape(
        fronts_here, rounds, tile_size, column_share * tile_size
    )
    front_slab = (slab_base[:, :, 0] + slab_cols) * live_rows[:, :, None, None]
    corner_tile = from_root(front_panel[:, 0], "grid", 0)
    factor = jnp.linalg.cholesky(corner_tile)
    solved = lax.linalg.triangular_solve(
        jnp.broadcast_to(factor[:, None], front_panel.shape),
        front_panel,
        left_side=False,
        lower=True,
        transpose_a=True,
    )
    first_tile = (tile_index == 0)[None, :, None, None]
    factored = jnp.where(first_tile, factor[:, None], solved)
    gathered = lax.all_gather(factored[:, :, None], "grid", axis=2, tiled=True)
    flattened = gathered.reshape(fronts_here, rounds * grid_size, tile_size, tile_size)
    wanted = lax.dynamic_slice_in_dim(flattened, 1 + depth_pos * column_share, column_share, 1)
    update = jnp.einsum("frai,fjbi->frajb", factored, wanted, precision=lax.Precision.HIGHEST)
    update = update.reshape(fronts_here, rounds, tile_size, column_share * tile_size)
    schur_block = front_slab - update
    return (factored[:, :, None], schur_block[:, :, None])


def solution(mesh):
    in_specs = (
        P("front", None, "grid", None, None),
        P("front", None, "grid", None, "depth"),
        P("front", "grid", "depth", None, None, None),
        P("front", "grid", "depth", None, None),
        P("front"),
    )
    out_specs = (P("front", None, "grid", None, None), P("front", None, "grid", None, "depth"))
    return jax.shard_map(
        on_device, mesh=mesh, in_specs=in_specs, out_specs=out_specs, check_vma=False
    )
```

profile of v0, /device:TPU:0, one launch (start us, length us, event | category | flops | bytes accessed | tf_op | source)
XLA Modules:
  0.0 504.1 jit_solution(17120897490595344676)
XLA Ops:
  7.2 0.8 add_bitcast_fusion
  7.9 0.7 and_select_fusion.2
  8.6 0.2 convert_reduce_fusion
  8.8 0.7 multiply_add_fusion.1
  9.5 0.2 convolution_bitcast_fusion.4
  9.7 0.6 copy.97
  10.3 5.2 %all-to-all-start = ((f32[1,4,2,20]{3,2,0,1:T(2,128)}), f32[1,4,2,20]{3,2,0,1:T(2,128)S(1)}, u32[]{:S(2)}, u32[]{:S(2)}) async-start(f32[1,4,2,20]{3,2,0,1:T(2,128)} %copy.97), calls=%async_computation | async-start | bytes 8192 | tf_op jit(solution)/shard_map/all_to_all | solution.py:46
  15.5 3.4 convolution_bitcast_fusion.1
  18.9 1.7 copy.100
  20.6 4.2 all-to-all-start.1
  24.8 0.1 reshape.543
  24.9 24.2 %all-to-all-done.1 = f32[1,4,2,256,256]{4,3,2,0,1:T(8,128)S(1)} async-done(((f32[1,4,2,256,256]{4,3,2,0,1:T(8,128)}), f32[1,4,2,256,256]{4,3,2,0,1:T(8,128)S(1)}, u32[]{:S(2)}, u32[]{:S(2)}) %all-to-all-start.1) | async-done | bytes 2097184 | tf_op jit(solution)/shard_map/all_to_all | solution.py:45
  49.1 9.7 %convolution_bitcast_fusion = f32[4,5,256,256]{3,1,2,0:T(8,128)} fusion(f32[1,4,2,256,256]{4,3,2,0,1:T(8,128)S(1)} %all-to-all-done.1, f32[4,5,2,4,1]{1,0,2,3,4:T(4,128)S(1)} %bitcast.130), kind=kOutput, calls=%fused_computation.2 | convolution fusion | flops 125829120 | bytes 7340672 | tf_op jit(solution)/shard_map/fskp,fskab->fpab/dot_general | solution.py:48
  58.9 8.6 %copy.103 = f32[4,5,256,256]{2,3,0,1:T(8,128)} copy(f32[4,5,256,256]{3,1,2,0:T(8,128)} %convolution_bitcast_fusion) | data formatting | bytes 10485760 | tf_op jit(solution)/shard_map/fskp,fskab->fpab/dot_general | solution.py:48
  67.5 4.6 slice.79
  72.0 2.4 slice_bitcast_fusion
  75.1 0.3 copy.96
  75.5 188.6 %all-reduce.7.cloned.1.call-done = (f32[1,4,256,256]{2,3,1,0:T(8,128)}, f32[1,4,4,256,256]{3,4,1,2,0:T(8,128)}) async-done(((f32[1,4,256,256]{2,3,1,0:T(8,128)}, f32[1,4,4,256,256]{3,4,1,2,0:T(8,128)}), (f32[1,4,256,256]{2,3,1,0:T(8,128)}, f32[1,4,4,256,256]{3,4,1,2,0:T(8,128)})) %all-reduce.7.cloned.1.call-update) | async-done | bytes 5242896 | tf_op jit(solution)/shard_map/psum | solution.py:54
  264.1 1.4 fusion.9
  265.5 0.7 fusion.15
  266.3 0.2 all-gather.2.cloned.1.call-start
  266.6 43.0 %all-reduce.5.cloned.1.call-done = f32[1,256,256]{1,2,0:T(8,128)} async-done(((f32[1,256,256]{1,2,0:T(8,128)}), f32[1,256,256]{1,2,0:T(8,128)}) %all-reduce.5.cloned.1.call-update) | async-done | bytes 262160 | tf_op jit(solution)/shard_map/psum | solution.py:11
  309.5 1.1 copy.104
  310.6 1.0 fusion.17
  311.6 11.7 %custom-call.16 = f32[1,128,128]{2,1,0:T(8,128)S(1)} custom-call(f32[1,128,128]{2,1,0:T(8,128)S(1)} %cholesky.114), custom_call_target="Cholesky" | custom-call | tf_op jit(solution)/shard_map/jit(cholesky)/cholesky | solution.py:64
  323.3 9.8 %custom-call.17 = f32[1,1,128,128]{2,3,1,0:T(8,128)S(1)} custom-call(f32[1,1,128,128]{3,2,1,0:T(8,128)S(1)} %get-tuple-element.37), custom_call_target="InvertDiagBlocksLowerTriangular" | custom-call | tf_op jit(solution)/shard_map/jit(cholesky)/cholesky | solution.py:64
  333.2 0.2 bitcast_dynamic-update-slice_fusion.1
  333.4 0.3 fusion.5
  333.7 11.7 %custom-call.18 = f32[1,128,128]{2,1,0:T(8,128)S(1)} custom-call(f32[1,128,128]{2,1,0:T(8,128)S(1)} %fusion.5), custom_call_target="Cholesky" | custom-call | tf_op jit(solution)/shard_map/jit(cholesky)/cholesky | solution.py:64
  345.4 0.6 compare_reduce_fusion
  347.3 0.1 copy.105
  347.6 5.5 %while.1 = (s32[]{:T(128)}, f32[1,4,256,256]{3,2,1,0:T(8,128)S(1)}, s32[2,2]{1,0:T(2,128)S(1)}, f32[2,1,4,128,128]{4,3,0,2,1:T(8,128)}, s32[]{:T(128)}) while((s32[]{:T(128)}, f32[1,4,256,256]{3,2,1,0:T(8,128)S(1)}, s32[2,2]{1,0:T(2,128)S(1)}, f32[2,1,4,128,128]{4,3,0,2,1:T(8,128)}, s32[]{:T(128)}) %tuple.33), condition=%wide.while_cond, body=%wide.while_body.sunk | while | flops 2 | bytes 525921 | solution.py:65
  347.8 0.6 fusion.42
  348.4 2.1 bitcast_dynamic-update-slice_fusion.3
  350.4 0.6 fusion.42
  351.0 2.1 bitcast_dynamic-update-slice_fusion.3
  353.1 79.4 %custom-call.19 = f32[1,4,2,128,128]{3,4,2,1,0:T(8,128)S(1)} custom-call(f32[1,4,2,128,128]{4,3,2,1,0:T(8,128)} %bitcast.135), custom_call_target="InvertDiagBlocksLowerTriangular" | custom-call | tf_op jit(solution)/shard_map/triangular_solve | solution.py:65
  432.5 0.6 fusion.11
  433.2 0.6 fusion.4
  433.8 0.6 fusion.14
  434.4 0.2 maximum_select_fusion
  434.6 1.4 copy.115
  436.0 2.5 copy.113
  438.6 1.3 copy.119
  439.9 49.0 %all-gather.2.cloned.1.call-done = f32[1,4,4,256,256]{4,3,1,0,2:T(8,128)} async-done(((f32[1,4,1,256,256]{4,3,1,0,2:T(8,128)}), f32[1,4,4,256,256]{4,3,1,0,2:T(8,128)}) %all-gather.2.cloned.1.call-update) | async-done | bytes 4194320 | tf_op jit(solution)/shard_map/all_gather | solution.py:74
  488.9 2.6 copy.116
  491.5 3.5 fusion.2
  495.0 2.5 copy.120
  (26 shorter events, 0.4 us)
Async XLA Ops:
  10.3 10.3 %all-to-all-start = ((f32[1,4,2,20]{3,2,0,1:T(2,128)}), f32[1,4,2,20]{3,2,0,1:T(2,128)S(1)}, u32[]{:S(2)}, u32[]{:S(2)}) async-start(f32[1,4,2,20]{3,2,0,1:T(2,128)} %copy.97), calls=%async_computation | async-start | bytes 8192 | tf_op jit(solution)/shard_map/all_to_all | solution.py:46
  20.6 28.5 %all-to-all-start.1 = ((f32[1,4,2,256,256]{4,3,2,0,1:T(8,128)}), f32[1,4,2,256,256]{4,3,2,0,1:T(8,128)S(1)}, u32[]{:S(2)}, u32[]{:S(2)}) async-start(f32[1,4,2,256,256]{4,3,2,0,1:T(8,128)} %copy.100), calls=%async_computation.1 | async-start | bytes 4194304 | tf_op jit(solution)/shard_map/all_to_all | solution.py:45
  24.8 239.3 %all-reduce.7.cloned.1.call-start = ((), (), s32[]{:S(2)}) async-start(), calls=%async_computation.4 | async-start | bytes 10485760 | tf_op jit(solution)/shard_map/psum | solution.py:54
  72.0 3.1 copy-start.1
  74.4 235.1 %all-reduce.5.cloned.1.call-start = ((), (), s32[]{:S(2)}) async-start(), calls=%async_computation.2 | async-start | bytes 524288 | tf_op jit(solution)/shard_map/psum | solution.py:11
  266.3 222.6 %all-gather.2.cloned.1.call-start = ((), (), s32[]{:S(2)}) async-start(), calls=%async_computation.3 | async-start | bytes 5242880 | tf_op jit(solution)/shard_map/all_gather | solution.py:74
  439.9 51.6 %copy-start = (f32[1,4,1,256,256]{3,4,1,2,0:T(8,128)S(1)}, f32[1,4,1,256,256]{3,4,1,2,0:T(8,128)}, u32[]{:S(2)}) copy-start(f32[1,4,1,256,256]{3,4,1,2,0:T(8,128)} %copy.113) | copy-start | bytes 3145732
Sparse Core Ops, SparseCore 0:
  74.6 189.4 all-reduce.6
  267.6 41.8 all-reduce.4
  436.1 52.6 all-gather.1
where the time goes:
time: 505 us; the launch traced here: 504 us
  waiting for transfers between devices  305 us (60%)
  other arithmetic  119 us (24%)
  local copies, waits for them, and re-layouts  35.3 us (7%)
  matrix products  19.3 us (4%)
  between operations  15.8 us (3%)
  starting transfers between devices  9.62 us (2%)
    psum x1, waiting for transfers between devices, on_device(): panel_sum, slab_sum = lax.psum((panel_part, slab_part), 'depth')  189 us
    another operation x4, other arithmetic, on_device(): lax.linalg.triangular_solve(jnp.broadcast_to(factor[:, None], front_panel...  79.5 us
    all_gather x1, waiting for transfers between devices, on_device(): gathered = lax.all_gather(factored[:, :, None], 'grid', axis=2, tiled=True)  49 us
    psum x1, waiting for transfers between devices, from_root(): return lax.psum(jnp.where(mine, x, jnp.zeros_like(x)), axis)  43 us
    another operation x6, other arithmetic, on_device(): factor = jnp.linalg.cholesky(corner_tile)  33.9 us
    all_to_all x1, waiting for transfers between devices, on_device(): lax.all_to_all(send_tiles, 'grid', split_axis=1, concat_axis=1, tiled=True)  24.2 us
  transfers between devices with their start and end apart: 5, of which 4 were waited for; matrix products, arithmetic and copies ran while one was open for 2% of the time, Pallas kernels for 0%

commit v1 on v0

v1 whole, which is shorter than its diff:
```python
import functools

import jax
import jax.numpy as jnp
from jax import lax
from jax.experimental import pallas as pl
from jax.experimental.pallas import tpu as pltpu
from jax.sharding import PartitionSpec as P

CAP = 2
CHUNK = 32
BLOCK = 64
HI = lax.Precision.HIGHEST


def dot(a, b, ca, cb):
    return lax.dot_general(
        a, b, (((ca,), (cb,)), ((), ())), precision=HI, preferred_element_type=jnp.float32
    )


def factor_block(w, b):
    tile = w.shape[0]
    s = b * BLOCK
    base = s // 128 * 128
    d = w[s : s + BLOCK, base : base + 128]
    if s != base:
        d = pltpu.roll(d, 128 - BLOCK, 1)
    row = lax.broadcasted_iota(jnp.int32, (BLOCK, 128), 0)
    lane = lax.broadcasted_iota(jnp.int32, (BLOCK, 128), 1)
    aug = jnp.where(lane < BLOCK, d, jnp.where(lane - BLOCK == row, 1.0, 0.0))

    def step(j, aug):
        at_row = jnp.where(row == j, aug, 0.0)
        at_both = jnp.where(lane == j, at_row, 0.0)
        col = jnp.sum(jnp.where(lane == j, aug, 0.0), axis=1, keepdims=True)
        pivot_row = jnp.sum(at_row, axis=0, keepdims=True)
        pivot = jnp.sum(jnp.sum(at_both, axis=0, keepdims=True), axis=1, keepdims=True)
        return jnp.where(row > j, aug - col * (pivot_row / pivot), aug)

    aug = lax.fori_loop(0, BLOCK, step, aug)
    diag = jnp.sum(jnp.where(lane == row, aug, 0.0), axis=1, keepdims=True)
    aug = aug / jnp.sqrt(diag)
    if s == base:
        inv = jnp.where(lane < BLOCK, pltpu.roll(aug, 128 - BLOCK, 1), 0.0)
    else:
        inv = jnp.where(lane >= BLOCK, aug, 0.0)
    rows = dot(inv, w[base : base + 128, :], 1, 0)
    w[s : s + BLOCK, :] = rows
    if s + BLOCK < tile:
        update = dot(rows[:, :tile], rows, 0, 0)
        w[s + BLOCK :, :] = w[s + BLOCK :, :] - update[s + BLOCK :, :]


def kernel(
    G, panel, slab, child, maps, orders, pout, sout,
    send, spos, recv, rpos, eslots, epos, cross_out, cross_in, mine, end_out, end_in,
    corner, fj, pf, w,
    corner_ss, corner_rs, pos_ss, pos_rs, a_ss, a_rs, ep_ss, ep_rs, e_ss, e_rs,
    c_ss, c_rs, t_ss, t_rs, f_ss, f_rs,
):
    R, tile, _ = panel.shape
    H = tile // CHUNK
    kids = child.shape[0]
    cols = 5
    g = lax.axis_index("grid")
    d = lax.axis_index("depth")
    is_mid = (d == 1) | (d == 2)
    is_end = (d == 0) | (d == 3)
    partner = d + 1 - 2 * (d % 2)
    other = 3 - d

    def peer(o):
        return (g + o) % G

    def copy(src, dst, ss, rs, axis, where):
        return pltpu.make_async_remote_copy(
            src_ref=src, dst_ref=dst, send_sem=ss, recv_sem=rs,
            device_id={axis: where}, device_id_type=pl.DeviceIdType.MESH,
        )

    barrier = pltpu.get_barrier_semaphore()
    for o in range(1, G):
        pl.semaphore_signal(barrier, inc=1, device_id={"grid": peer(o)}, device_id_type=pl.DeviceIdType.MESH)
    for o in range(1, 4):
        pl.semaphore_signal(barrier, inc=1, device_id={"depth": (d + o) % 4}, device_id_type=pl.DeviceIdType.MESH)
    pl.semaphore_wait(barrier, G - 1 + 3)

    def corner_copy(o):
        return copy(panel.at[0], corner, corner_ss.at[o], corner_rs, "grid", peer(o))

    @pl.when(g == 0)
    def _():
        for o in range(1, G):
            corner_copy(o).start()

    prow = [maps[k, 0] for k in range(kids)]
    pcol = [maps[k, 1] for k in range(kids)]
    owner = [x % G for x in prow]
    rank = []
    for k in range(kids):
        n = jnp.int32(0)
        for i in range(k):
            n = n + (owner[i] == owner[k]).astype(jnp.int32)
        rank.append(n)
    for o in [*range(1, G), 0]:
        to, to_pos = (recv, rpos) if o == 0 else (send, spos)
        for s in range(CAP):
            which, place = jnp.int32(0), jnp.int32(-1)
            for k in range(kids):
                hit = (owner[k] == peer(o)) & (rank[k] == s)
                which = jnp.where(hit, k, which)
                place = jnp.where(hit, prow[k] // G * cols + pcol[k], place)
            to_pos[CAP * o + s] = jnp.full((8, 128), place.astype(jnp.float32))

            def move(h, _):
                rows = pl.ds(pl.multiple_of(h * CHUNK, CHUNK), CHUNK)
                to[h, CAP * o + s] = child[which, rows, :]
                return 0

            lax.fori_loop(0, H, move, 0)

    def pos_copy(o):
        two = pl.ds(CAP * o, CAP)
        return copy(spos.at[two], rpos.at[two], pos_ss.at[o], pos_rs.at[o], "grid", peer(o))

    def a_copy(o, h):
        two = pl.ds(CAP * o, CAP)
        return copy(send.at[h, two], recv.at[h, two], a_ss.at[o, h], a_rs.at[o, h], "grid", peer(o))

    def epos_copy():
        return copy(rpos, epos, ep_ss, ep_rs, "depth", partner)

    def e_copy(h):
        return copy(recv.at[h], eslots.at[h], e_ss.at[h], e_rs.at[h], "depth", partner)

    def c_copy(h):
        return copy(cross_out.at[h], cross_in.at[h], c_ss.at[h], c_rs.at[h], "depth", other)

    def t_copy(h):
        return copy(end_out.at[h], end_in.at[h], t_ss.at[h], t_rs.at[h], "depth", partner)

    for o in range(1, G):
        pos_copy(o).start()
    for h in range(H):
        for o in range(1, G):
            a_copy(o, h).start()

    @pl.when(g == 0)
    def _():
        w[:, :tile] = panel[0]

    @pl.when(g != 0)
    def _():
        corner_copy(1).wait_recv()
        w[:, :tile] = corner[...]

    ii = lax.broadcasted_iota(jnp.int32, (tile, tile), 0)
    jj = lax.broadcasted_iota(jnp.int32, (tile, tile), 1)
    w[:, tile:] = jnp.where(ii == jj, 1.0, 0.0)

    for o in range(1, G):
        pos_copy(o).wait_recv()

    @pl.when(is_end)
    def _():
        epos_copy().start()

    @pl.when(is_mid)
    def _():
        epos_copy().wait_recv()

    def spread(h):
        far = [(r * cols + c).astype(jnp.float32) for c in (other + 1, 3 - partner + 1) for r in range(R)]
        near = [(r * cols + c).astype(jnp.float32) for c in (d + 1, partner + 1) for r in range(R)]
        mid = [jnp.float32(r * cols) for r in range(R)]
        wanted = far + near + mid

        def part(q, _):
            rows = pl.ds(pl.multiple_of(q * 8, 8), 8)
            for half in range(tile // 128):
                lanes = pl.ds(half * 128, 128)
                acc = [jnp.zeros((8, 128), jnp.float32) for _ in wanted]
                for data, pos in ((recv, rpos), (eslots, epos)):
                    for s in range(G * CAP):
                        x, where = data[h, s, rows, lanes], pos[s]
                        for p in range(len(wanted)):
                            acc[p] = acc[p] + jnp.where(where == wanted[p], x, 0.0)
                for p in range(2 * R):
                    cross_out[h, p, rows, lanes] = acc[p]
                    mine[h, p, rows, lanes] = acc[2 * R + p]
                for r in range(R):
                    cross_out[h, 2 * R + r, rows, lanes] = acc[4 * R + r]
                    mine[h, 2 * R + r, rows, lanes] = acc[4 * R + r]
            return 0

        lax.fori_loop(0, CHUNK // 8, part, 0)

    def stage_a(h):
        for o in range(1, G):
            a_copy(o, h).wait_recv()

        @pl.when(is_end)
        def _():
            e_copy(h).start()

        @pl.when(is_mid)
        def _():
            e_copy(h).wait_recv()
            spread(h)
            c_copy(h).start()

    row_j, owner_j = (d + 1) // G, (d + 1) % G

    def f_copy(o, h):
        rows = pl.ds(h * CHUNK, CHUNK)
        return copy(pf.at[row_j, rows], fj.at[rows], f_ss.at[o, h], f_rs.at[h], "grid", peer(o))

    def close(h, sums):
        rows = pl.ds(h * CHUNK, CHUNK)
        for r in range(R):
            slab_sum, panel_sum = sums(r)
            live = ((r * G + g) * tile < orders[0]).astype(jnp.float32)
            pf[r, rows, :] = (panel[r, rows, :] + panel_sum) * live
            sout[r, rows, :] = (slab[r, rows, :] + slab_sum) * live

        @pl.when(g == owner_j)
        def _():
            for o in range(1, G):
                f_copy(o, h).start()
            fj[rows, :] = pf[row_j, rows, :]

    def stage_b(h):
        @pl.when(is_mid)
        def _():
            c_copy(h).wait_recv()
            for r in range(R):
                end_out[h, r] = mine[h, R + r] + cross_in[h, R + r]
                end_out[h, R + r] = mine[h, 2 * R + r] + cross_in[h, 2 * R + r]
            t_copy(h).start()
            close(h, lambda r: (mine[h, r] + cross_in[h, r], end_out[h, R + r]))

    def stage_c(h):
        @pl.when(is_end)
        def _():
            t_copy(h).wait_recv()
            close(h, lambda r: (end_in[h, r], end_in[h, R + r]))

    blocks = tile // BLOCK
    per = H // blocks
    for b in range(blocks):
        for h in range(b * per, (b + 1) * per):
            stage_a(h)
        if b >= 1:
            for h in range((b - 1) * per, b * per):
                stage_b(h)
        factor_block(w, b)
    for h in range((blocks - 1) * per, H):
        stage_b(h)
    factor = jnp.where(ii >= jj, w[:, :tile].T, 0.0)
    inverse = jnp.where(ii >= jj, w[:, tile:], 0.0)
    for h in range(H):
        stage_c(h)

    for r in range(R):
        solved = dot(pf[r], inverse, 1, 1)
        if r == 0:
            solved = jnp.where(g == 0, factor, solved)
        pout[r] = solved

    @pl.when(g != owner_j)
    def _():
        for h in range(H):
            f_copy(1, h).wait_recv()

    wanted = dot(fj[...], inverse, 1, 1)
    for r in range(R):
        sout[r] = sout[r] - dot(pout[r], wanted, 1, 1)

    @pl.when(g == 0)
    def _():
        for o in range(1, G):
            corner_copy(o).wait_send()

    for o in range(1, G):
        pos_copy(o).wait_send()
        for h in range(H):
            a_copy(o, h).wait_send()

    @pl.when(is_end)
    def _():
        epos_copy().wait_send()
        for h in range(H):
            e_copy(h).wait_send()

    @pl.when(is_mid)
    def _():
        for h in range(H):
            c_copy(h).wait_send()
            t_copy(h).wait_send()

    @pl.when(g == owner_j)
    def _():
        for o in range(1, G):
            for h in range(H):
                f_copy(o, h).wait_send()


def on_device(G, panel_base, slab_base, child_tiles, child_maps, front_orders):
    R, tile = panel_base.shape[1], panel_base.shape[3]
    kids = child_tiles.shape[3]
    H = tile // CHUNK
    slots = G * CAP
    f32 = jnp.float32
    vm = lambda *shape: pltpu.VMEM(shape, f32)
    sem = lambda *shape: pltpu.SemaphoreType.DMA(shape)
    one = pltpu.SemaphoreType.DMA
    vmem = pl.BlockSpec(memory_space=pltpu.VMEM)
    smem = pl.BlockSpec(memory_space=pltpu.SMEM)
    pout, sout = pl.pallas_call(
        functools.partial(kernel, G),
        out_shape=[jax.ShapeDtypeStruct((R, tile, tile), f32)] * 2,
        in_specs=[vmem, vmem, vmem, smem, smem],
        out_specs=[vmem, vmem],
        scratch_shapes=[
            vm(H, slots, CHUNK, tile), vm(slots, 8, 128),
            vm(H, slots, CHUNK, tile), vm(slots, 8, 128),
            vm(H, slots, CHUNK, tile), vm(slots, 8, 128),
            vm(H, 3 * R, CHUNK, tile), vm(H, 3 * R, CHUNK, tile), vm(H, 3 * R, CHUNK, tile),
            vm(H, 2 * R, CHUNK, tile), vm(H, 2 * R, CHUNK, tile),
            vm(tile, tile), vm(tile, tile), vm(R, tile, tile), vm(tile, 2 * tile),
            sem(G), one, sem(G), sem(G), sem(G, H), sem(G, H), one, one, sem(H), sem(H),
            sem(H), sem(H), sem(H), sem(H), sem(G, H), sem(H),
        ],
        compiler_params=pltpu.CompilerParams(
            collective_id=0, has_side_effects=True, vmem_limit_bytes=50 * 1024 * 1024
        ),
    )(
        panel_base.reshape(R, tile, tile),
        slab_base.reshape(R, tile, tile),
        child_tiles.reshape(kids, tile, tile),
        child_maps.reshape(kids, 2),
        front_orders,
    )
    return pout.reshape(panel_base.shape), sout.reshape(slab_base.shape)


def solution(mesh):
    in_specs = (
        P("front", None, "grid", None, None),
        P("front", None, "grid", None, "depth"),
        P("front", "grid", "depth", None, None, None),
        P("front", "grid", "depth", None, None),
        P("front"),
    )
    out_specs = (P("front", None, "grid", None, None), P("front", None, "grid", None, "depth"))
    return jax.shard_map(
        functools.partial(on_device, mesh.shape["grid"]),
        mesh=mesh, in_specs=in_specs, out_specs=out_specs, check_vma=False,
    )
```

time: 505 us -> 116 us (0.23)
  waiting for transfers between devices: 305 us -> 0 us
  other arithmetic: 119 us -> 0 us
  Pallas kernels: 0 us -> 110 us
  local copies, waits for them, and re-layouts: 35.3 us -> 3.93 us
  matrix products: 19.3 us -> 0 us
  between operations: 15.8 us -> 1.3 us
  starting transfers between devices: 9.62 us -> 0 us
    psum x2 -> x0, waiting for transfers between devices: 232 us -> none  [the longest x1 189 us: on_device(): panel_sum, slab_sum = lax.psum((panel_part, slab_part), 'depth')]
    another operation x10 -> x0, other arithmetic: 113 us -> none  [the longest x4 79.5 us: on_device(): lax.linalg.triangular_solve(jnp.broadcast_to(factor[:, None], front_panel...]
    pallas_call x0 -> x1, Pallas kernels: none -> 110 us  [on_device(): pl.pallas_call(functools.partial(kernel, G), out_shape=[jax.ShapeDtypeStr...]
    all_gather x1 -> x0, waiting for transfers between devices: 49 us -> none  [on_device(): gathered = lax.all_gather(factored[:, :, None], 'grid', axis=2, tiled=True)]
    all_to_all x2 -> x0, waiting for transfers between devices: 24.2 us -> none  [the longest x1 24.2 us: on_device(): lax.all_to_all(send_tiles, 'grid', split_axis=1, concat_axis=1, tiled=True)]
    dot_general x4 -> x0, matrix products: 16.9 us -> none  [the longest x1 9.74 us: on_device(): jnp.einsum('fskp,fskab->fpab', arrived_places, arrived, precision=lax.Pre...]
    dot_general x3 -> x0, local copies, waits for them, and re-layouts: 10.9 us -> none  [the longest x1 8.62 us: on_device(): jnp.einsum('fskp,fskab->fpab', arrived_places, arrived, precision=lax.Pre...]
    all_to_all x2 -> x0, starting transfers between devices: 9.36 us -> none  [the longest x1 5.16 us: on_device(): lax.all_to_all(send_places, 'grid', split_axis=1, concat_axis=1, tiled=True)]
  transfers between devices with their start and end apart: 5 -> 0, of which waited for: 4 -> 0; matrix products, arithmetic and copies ran while one was open for 2% -> 0% of each run, Pallas kernels for 0% -> 0%
where the time goes in v1:
time: 116 us
  Pallas kernels  110 us (95%)
  local copies, waits for them, and re-layouts  3.93 us (3%)
  between operations  1.3 us (1%)
    pallas_call x1, Pallas kernels, on_device(): pl.pallas_call(functools.partial(kernel, G), out_shape=[jax.ShapeDtypeStr...  110 us
    unnamed x6, local copies, waits for them, and re-layouts  3.84 us

profile of v1, /device:TPU:0, one launch (start us, length us, event | category | flops | bytes accessed | tf_op | source)
XLA Modules:
  0.0 115.6 jit_solution(9467533255959418131)
XLA Ops:
  1.3 0.0 copy-start.1
  1.3 0.7 copy-done.1
  2.0 0.1 copy.7.maps
  2.0 0.0 copy-start
  2.1 1.2 %copy-done = f32[1,4,1,256,256]{4,3,2,1,0:T(8,128)S(1)} copy-done((f32[1,4,1,256,256]{4,3,2,1,0:T(8,128)S(1)}, f32[1,4,1,256,256]{4,3,2,1,0:T(8,128)}, u32[]{:S(2)}) %copy-start) | copy-done | bytes 1048600
  3.3 110.3 %shard_map.68 = (f32[4,256,256]{2,1,0:T(8,128)S(1)}, f32[4,256,256]{2,1,0:T(8,128)S(1)}) custom-call(f32[4,256,256]{2,1,0:T(8,128)S(1)} %bitcast.10, f32[4,256,256]{2,1,0:T(8,128)} %bitcast.13, f32[4,256,256]{2,1,0:T(8,128)} %bitcast.14, s32[4,2]{1,0:T(4,128)S(1)} %copy.7.maps, s32[1]{0:T(128)S(6)} %copy.12.orders), custom_call_target="tpu_custom_call" | custom-call | tf_op jit(solution)/shard_map/pallas_call | solution.py:320
  113.6 1.0 copy.13
  114.6 1.0 copy.14
Async XLA Ops:
  1.3 0.7 copy-start.1
  2.0 1.2 %copy-start = (f32[1,4,1,256,256]{4,3,2,1,0:T(8,128)S(1)}, f32[1,4,1,256,256]{4,3,2,1,0:T(8,128)}, u32[]{:S(2)}) copy-start(f32[1,4,1,256,256]{4,3,2,1,0:T(8,128)} %param.5) | copy-start | bytes 3145732
